TPU v7x, 512 devices: a whole 4x8x8 slice. The times are simulated.
512 devices in a mesh: dp: 16 (over y, core), slab: 16 (over z, x_lo), chan: 2 (over x_hi).
Axes of the slice: x: 4 (x_hi: 2, x_lo: 2; x = x_hi * 2 + x_lo), y: 8, z: 8, core: 2. Of those that a mesh axis runs over, the one named last changes fastest.
Arguments:
- center_in: bfloat16 [16, 64, 128, 256], P('dp', 'slab', None, 'chan'), may hold values from 0 to 2
- radius_in: bfloat16 [16, 64, 128, 256], P('dp', 'slab', None, 'chan'), may hold values from 0.049804688 to 1
- hidden_center: bfloat16 [16, 64, 128, 256], P('dp', 'slab', None, 'chan'), may hold values from 0 to 2
- hidden_radius: bfloat16 [16, 64, 128, 256], P('dp', 'slab', None, 'chan'), may hold values from 0 to 1
- state_one: int32 [16, 64, 128, 256], P('dp', 'slab', None, 'chan'), may hold values from 0 to 2
- state_two: int32 [16, 64, 128, 256], P('dp', 'slab', None, 'chan'), may hold values from 0 to 2
- weight_one: bfloat16 [3, 3, 256, 256], P(None, None, None, 'chan'), may hold values from -0.125 to 0.125
- weight_two: bfloat16 [3, 3, 256, 256], P(None, None, None, 'chan'), may hold values from -0.125 to 0.125
- grad_center: bfloat16 [16, 64, 128, 256], P('dp', 'slab', None, 'chan'), may hold values from -6 to 6
- grad_radius: bfloat16 [16, 64, 128, 256], P('dp', 'slab', None, 'chan'), may hold values from -6 to 6
Outputs:
- input_grad_center: float32 [16, 64, 128, 256], P('dp', 'slab', None, 'chan')
- input_grad_radius: float32 [16, 64, 128, 256], P('dp', 'slab', None, 'chan')
- kernel_grad_one: bfloat16 [3, 3, 256, 256], P(None, None, None, 'chan')
- kernel_grad_two: bfloat16 [3, 3, 256, 256], P(None, None, None, 'chan')
Inputs may be any that keep to these rules, and one draw needn't show every extreme that they name: `state_one`: 0 marks an inactive unit, 1 an active one, 2 an unstable one. `state_two`: 0 marks an inactive unit, 1 an active one, 2 an unstable one.
All inputs are finite; a program needn't handle non-finite values.
Results may differ from a plain program's by a relative error of at most 0.0054.
Values may be sent and summed in bfloat16 or wider, within the bound.
A program may use at most 64 MiB of HBM per device.

v0:
```python
import math

import jax
import jax.numpy as jnp
from jax import lax
from jax.sharding import PartitionSpec as P


def with_halo(block, sides, width):
    for axis, dim in sides:
        count = lax.axis_size(axis)
        forward = [(i, i + 1) for i in range(count - 1)]
        backward = [(target, source) for source, target in forward]
        low = lax.ppermute(
            lax.slice_in_dim(block, block.shape[dim] - width, None, axis=dim), axis, forward
        )
        high = lax.ppermute(lax.slice_in_dim(block, 0, width, axis=dim), axis, backward)
        block = jnp.concatenate([low, block, high], axis=dim)
    return block


def relu_back(grad_c, grad_r, states):
    average = 0.5 * (grad_c + grad_r)
    keep_c = jnp.where(states == 1, grad_c, jnp.where(states == 2, average, 0.0))
    keep_r = jnp.where(states == 1, grad_r, jnp.where(states == 2, average, 0.0))
    return (keep_c.astype(jnp.bfloat16), keep_r.astype(jnp.bfloat16))


def total_over(values):
    return lax.psum(values, ("dp", "slab"))


def layer_back(grad_c, grad_r, act_c, act_r, weight, loss_scale):
    stacked = jnp.stack((grad_c, grad_r))
    halo_rows = with_halo(stacked, (("slab", 2),), 1)
    padded = jnp.pad(halo_rows, ((0, 0), (0, 0), (0, 0), (1, 1), (0, 0)))
    row_count, col_count = (grad_c.shape[1], grad_c.shape[2])
    weight_sign = jnp.sign(weight).astype(jnp.float32)
    magnitude = jnp.abs(weight)
    out_shape = grad_c.shape[:3] + (weight.shape[2],)
    back_c = jnp.zeros(out_shape, jnp.float32)
    back_r = jnp.zeros(out_shape, jnp.float32)
    taps_c = []
    taps_r = []
    for row_tap in range(3):
        for col_tap in range(3):
            window = padded[
                :,
                :,
                2 - row_tap : 2 - row_tap + row_count,
                2 - col_tap : 2 - col_tap + col_count,
                :,
            ]
            full_window = padded[
                :,
                :,
                2 - row_tap : 2 - row_tap + row_count,
                2 - col_tap : 2 - col_tap + col_count,
                :,
            ]
            back_c = back_c + jnp.einsum(
                "bhwo,io->bhwi",
                full_window[0],
                weight[row_tap, col_tap],
                preferred_element_type=jnp.float32,
            )
            back_r = back_r + jnp.einsum(
                "bhwo,io->bhwi",
                full_window[1],
                magnitude[row_tap, col_tap],
                preferred_element_type=jnp.float32,
            )
            taps_c.append(
                jnp.einsum("bhwi,bhwo->io", act_c, window[0], preferred_element_type=jnp.float32)
            )
            taps_r.append(
                jnp.einsum("bhwi,bhwo->io", act_r, window[1], preferred_element_type=jnp.float32)
            )
    center_taps = jnp.stack(taps_c).reshape(weight.shape)
    radius_taps = jnp.stack(taps_r).reshape(weight.shape)
    kernel_terms = loss_scale * (center_taps + weight_sign * radius_taps)
    summed = total_over(kernel_terms)
    back_c, back_r = (
        lax.psum_scatter(back_c, "chan", scatter_dimension=3, tiled=True),
        lax.psum_scatter(back_r, "chan", scatter_dimension=3, tiled=True),
    )
    return (back_c, back_r, summed.astype(jnp.bfloat16))


def body(
    center_in,
    radius_in,
    hidden_center,
    hidden_radius,
    state_one,
    state_two,
    weight_one,
    weight_two,
    grad_center,
    grad_radius,
):
    full_center, full_radius, full_hidden_c, full_hidden_r = (
        lax.all_gather(center_in, "chan", axis=3, tiled=True),
        lax.all_gather(radius_in, "chan", axis=3, tiled=True),
        lax.all_gather(hidden_center, "chan", axis=3, tiled=True),
        lax.all_gather(hidden_radius, "chan", axis=3, tiled=True),
    )
    pixels = (
        grad_center.shape[0]
        * grad_center.shape[1]
        * grad_center.shape[2]
        * lax.axis_size("dp")
        * lax.axis_size("slab")
    )
    loss_scale = 1.0 / math.sqrt(pixels)
    skip_c, skip_r = relu_back(
        grad_center.astype(jnp.float32), grad_radius.astype(jnp.float32), state_two
    )
    back_c, back_r, kernel_two = layer_back(
        skip_c, skip_r, full_hidden_c, full_hidden_r, weight_two, loss_scale
    )
    inner_c, inner_r = relu_back(back_c, back_r, state_one)
    back_c, back_r, kernel_one = layer_back(
        inner_c, inner_r, full_center, full_radius, weight_one, loss_scale
    )
    return (
        skip_c.astype(jnp.float32) + back_c,
        skip_r.astype(jnp.float32) + back_r,
        kernel_one,
        kernel_two,
    )


def solution(mesh):
    in_specs = (
        P("dp", "slab", None, "chan"),
        P("dp", "slab", None, "chan"),
        P("dp", "slab", None, "chan"),
        P("dp", "slab", None, "chan"),
        P("dp", "slab", None, "chan"),
        P("dp", "slab", None, "chan"),
        P(None, None, None, "chan"),
        P(None, None, None, "chan"),
        P("dp", "slab", None, "chan"),
        P("dp", "slab", None, "chan"),
    )
    out_specs = (
        P("dp", "slab", None, "chan"),
        P("dp", "slab", None, "chan"),
        P(None, None, None, "chan"),
        P(None, None, None, "chan"),
    )
    return jax.shard_map(body, mesh=mesh, in_specs=in_specs, out_specs=out_specs, check_vma=False)
```

profile of v0, /device:TPU:1, one launch (start us, length us, event | category | flops | bytes accessed | tf_op | source)
XLA Modules:
  0.0 1265.3 jit_solution(17248352069651281494)
XLA Ops:
  7.2 1.3 fusion.55
  8.5 1.1 fusion.58
  9.6 4.1 collective-permute-start
  13.7 1.4 collective-permute-start.1
  15.2 7.6 all_gather.15
  22.8 6.7 all_gather.14
  29.7 6.0 all_gather.13
  36.7 6.0 all_gather.12
  43.3 1.0 fusion.107
  54.0 1.3 convolution_add_fusion.27
  57.3 1.0 fusion.1
  58.4 1.6 fusion.24
  63.6 2.7 copy.52
  69.8 2.7 copy.53
  72.5 16.0 %reduce-scatter.7.cloned.1.call-done = f32[1,4,128,128]{3,2,1,0:T(8,128)} async-done(((f32[1,4,128,256]{3,2,1,0:T(8,128)}), f32[1,4,128,128]{3,2,1,0:T(8,128)}) %reduce-scatter.7.cloned.1.call-update) | async-done | bytes 262160 | tf_op jit(solution)/shard_map/reduce_scatter | solution.py:85
  88.5 27.0 %reduce-scatter.5.cloned.1.call-done = f32[1,4,128,128]{3,2,1,0:T(8,128)} async-done(((f32[1,4,128,256]{3,2,1,0:T(8,128)}), f32[1,4,128,128]{3,2,1,0:T(8,128)}) %reduce-scatter.5.cloned.1.call-update) | async-done | bytes 262160 | tf_op jit(solution)/shard_map/reduce_scatter | solution.py:84
  115.5 1.2 select_convert_fusion.1
  116.8 1.0 select_convert_fusion
  117.8 2.2 collective-permute-start.2
  120.1 1.3 collective-permute-start.3
  121.4 1.7 add_multiply_fusion
  123.1 2.8 collective-permute-done.3
  126.0 1.9 fusion.113
  127.9 1.8 fusion.114
  133.9 2.7 copy.32
  139.7 2.7 copy.33
  142.4 3.2 add_multiply_fusion.1
  148.6 1.3 convolution_add_fusion.13
  151.3 1.0 fusion.5
  152.3 1103.1 %all-reduce.4 = (bf16[3,3,256,128]{3,2,1,0:T(8,128)(2,1)}, bf16[3,3,256,128]{3,2,1,0:T(8,128)(2,1)}) all-reduce(f32[3,3,256,128]{3,2,1,0:T(8,128)} %add_multiply_fusion.1, f32[3,3,256,128]{3,2,1,0:T(8,128)S(1)} %add_multiply_fusion), channel_id=1, replica_groups=mesh['dp'=16,'slab'=16,'chan'=2] {'dp','slab'}, use_global_device_ids=true, to_apply=%region_4.5 | all-reduce | flops 589824 | bytes 3538944 | tf_op jit(solution)/shard_map/psum | solution.py:30
  1255.4 1.7 convert_add_fusion.1
  1257.1 1.7 convert_add_fusion.2
  (113 shorter events, 32.1 us)
Async XLA Ops:
  7.2 8.0 copy-start.11
  7.2 15.6 %copy-start.12 = (bf16[1,4,128,128]{3,2,1,0:T(8,128)(2,1)S(1)}, bf16[1,4,128,128]{3,2,1,0:T(8,128)(2,1)}, u32[]{:S(2)}) copy-start(bf16[1,4,128,128]{3,2,1,0:T(8,128)(2,1)} %param.12) | copy-start | bytes 393220
  7.2 22.4 %copy-start = (bf16[3,3,256,128]{3,2,1,0:T(8,128)(2,1)S(1)}, bf16[3,3,256,128]{3,2,1,0:T(8,128)(2,1)}, u32[]{:S(2)}) copy-start(bf16[3,3,256,128]{3,2,1,0:T(8,128)(2,1)} %param.17) | copy-start | bytes 1769476
  7.2 81.3 %reduce-scatter.7.cloned.1.call-start = ((), (), s32[]{:S(2)}) async-start(), calls=%async_computation.5 | async-start | bytes 786432 | tf_op jit(solution)/shard_map/reduce_scatter | solution.py:85
  9.6 20.1 %copy-start.13 = (bf16[1,4,128,128]{3,2,1,0:T(8,128)(2,1)S(1)}, bf16[1,4,128,128]{3,2,1,0:T(8,128)(2,1)}, u32[]{:S(2)}) copy-start(bf16[1,4,128,128]{3,2,1,0:T(8,128)(2,1)} %param.11) | copy-start | bytes 393220
  9.6 33.0 %collective-permute-start = (bf16[2,1,1,128,128]{4,3,2,1,0:T(8,128)(2,1)S(1)}, bf16[2,1,1,128,128]{4,3,2,1,0:T(8,128)(2,1)S(1)}, u32[]{:S(2)}, u32[]{:S(2)}) collective-permute-start(bf16[2,1,1,128,128]{4,3,2,1,0:T(8,128)(2,1)S(1)} %get-tuple-element.14), channel_id=1, source_target_pairs={{0,2},{2,4},{4,6},{6,8},{8,10},{10,12},{12,14},{14,16},{16,18},{18... | collective-permute-start | bytes 196616 | tf_op jit(solution)/shard_map/ppermute | solution.py:14
  13.7 22.0 %copy-start.1 = (bf16[3,3,256,128]{3,2,1,0:T(8,128)(2,1)S(1)}, bf16[3,3,256,128]{3,2,1,0:T(8,128)(2,1)}, u32[]{:S(2)}) copy-start(bf16[3,3,256,128]{3,2,1,0:T(8,128)(2,1)} %param.16) | copy-start | bytes 1769476
  13.7 29.0 %collective-permute-start.1 = (bf16[2,1,1,128,128]{4,3,2,1,0:T(8,128)(2,1)S(1)}, bf16[2,1,1,128,128]{4,3,2,1,0:T(8,128)(2,1)S(1)}, u32[]{:S(2)}, u32[]{:S(2)}) collective-permute-start(bf16[2,1,1,128,128]{4,3,2,1,0:T(8,128)(2,1)S(1)} %get-tuple-element.15), channel_id=1, source_target_pairs={{2,0},{4,2},{6,4},{8,6},{10,8},{12,10},{14,12},{16,14},{18,16},{20... | collective-permute-start | bytes 196616 | tf_op jit(solution)/shard_map/ppermute | solution.py:17
  29.6 7.1 copy-start.14
  42.7 8.9 copy-start.6
  54.0 61.6 %reduce-scatter.5.cloned.1.call-start = ((), (), s32[]{:S(2)}) async-start(), calls=%async_computation.4 | async-start | bytes 786432 | tf_op jit(solution)/shard_map/reduce_scatter | solution.py:84
  62.7 1192.8 %reduce-scatter.11.cloned.1.call-start = ((), (), s32[]{:S(2)}) async-start(), calls=%async_computation.7 | async-start | bytes 786432 | tf_op jit(solution)/shard_map/reduce_scatter | solution.py:85
  69.8 45.7 %copy-start.10 = (s32[1,4,128,128]{3,2,1,0:T(8,128)S(1)}, s32[1,4,128,128]{3,2,1,0:T(8,128)}, u32[]{:S(2)}) copy-start(s32[1,4,128,128]{3,2,1,0:T(8,128)} %param.14) | copy-start | bytes 786436
  88.5 28.3 %copy-start.9 = (f32[1,4,128,128]{3,2,1,0:T(8,128)S(1)}, f32[1,4,128,128]{3,2,1,0:T(8,128)}, u32[]{:S(2)}) copy-start(f32[1,4,128,128]{3,2,1,0:T(8,128)} %reduce-scatter.7.cloned.1.call-done) | copy-start | bytes 786436
  115.5 5.8 copy-start.2
  117.8 5.2 collective-permute-start.2
  120.1 5.8 collective-permute-start.3
  132.8 1.0 copy-start.7
  138.6 1.0 copy-start.8
  142.3 3.2 copy-start.3
  142.3 3.2 copy-start.5
  146.5 1.0 copy-start.4
  148.6 1108.6 %reduce-scatter.9.cloned.1.call-start = ((), (), s32[]{:S(2)}) async-start(), calls=%async_computation.6 | async-start | bytes 786432 | tf_op jit(solution)/shard_map/reduce_scatter | solution.py:84
Sparse Core Ops, SparseCore 0:
  54.1 34.3 reduce-scatter.6
  92.1 23.3 reduce-scatter.4
  148.7 27.2 reduce-scatter.10
  178.8 24.3 reduce-scatter.8
where the time goes:
time: 1290 us; the launch traced here: 1270 us
  blocking collectives  1130 us (88%)
  waiting for transfers between devices  45.9 us (4%)
  matrix products  38.9 us (3%)
  between operations  14.3 us (1%)
  other arithmetic  14.2 us (1%)
  local copies, waits for them, and re-layouts  13.4 us (1%)
    psum x1, blocking collectives, total_over(): return lax.psum(values, ('dp', 'slab'))  1100 us
    reduce_scatter x2, waiting for transfers between devices, layer_back(): lax.psum_scatter(back_c, 'chan', scatter_dimension=3, tiled=True)  27 us
  transfers between devices with their start and end apart: 8, of which 3 were waited for; matrix products, arithmetic and copies ran while one was open for 2% of the time, Pallas kernels for 0%

commit v1 on v0

v1 whole, which is shorter than its diff:
```python
import functools
import math

import jax
import jax.numpy as jnp
from jax import lax
from jax.experimental import pallas as pl
from jax.experimental.pallas import tpu as pltpu
from jax.sharding import PartitionSpec as P

MESH = pl.DeviceIdType.MESH
F32 = jnp.float32
BF16 = jnp.bfloat16


def relu_back(grad_c, grad_r, states):
    average = 0.5 * (grad_c + grad_r)
    keep_c = jnp.where(states == 1, grad_c, jnp.where(states == 2, average, 0.0))
    keep_r = jnp.where(states == 1, grad_r, jnp.where(states == 2, average, 0.0))
    return keep_c.astype(BF16), keep_r.astype(BF16)


def kernel(
    sizes,
    center_in,
    radius_in,
    hidden_center,
    hidden_radius,
    state_one,
    state_two,
    weight_one,
    weight_two,
    grad_center,
    grad_radius,
    out_c,
    out_r,
    out_k,
    grads,
    states,
    wcat,
    wabs,
    act,
    act_t,
    skip,
    inner,
    halo,
    cols,
    part_own,
    part_send,
    part_recv,
    final,
    k_full,
    k_send,
    k_recv,
    k_mine,
    got_one,
    two,
    got_two,
    result,
    in_sem,
    w_sem,
    act_sem,
    halo_ss,
    halo_rs,
    act_ss,
    act_rs,
    part_ss,
    part_rs,
    core_sem,
    one_ss,
    one_rs,
    two_ss,
    two_rs,
    back_ss,
    back_rs,
    fwd_ss,
    fwd_rs,
    out_sem,
    k_out_sem,
):
    ny, nz, rows, width, scale = sizes
    pix = rows * width
    dp, slab, chan = lax.axis_index("dp"), lax.axis_index("slab"), lax.axis_index("chan")
    y, core = lax.div(dp, 2), lax.rem(dp, 2)
    z, x_lo = lax.div(slab, 2), lax.rem(slab, 2)
    slabs = 2 * nz
    first = core == 0
    members = 2 * ny
    chunk = 256 // members
    pos_one = jnp.where(first, y, z) * 2 + x_lo
    pos_two = jnp.where(first, z, y)

    def one_dev(j):
        a = lax.div(j, 2)
        return (
            jnp.where(first, a, y) * 2 + core,
            jnp.where(first, z, a) * 2 + lax.rem(j, 2),
            chan,
        )

    def two_dev(j):
        return (jnp.where(first, y, j) * 2 + core, jnp.where(first, j, z) * 2 + x_lo, chan)

    partner = (dp, slab, 1 - chan)
    sibling = (y * 2 + 1 - core, slab, chan)
    above = (dp, lax.rem(slab + slabs - 1, slabs), chan)
    below = (dp, lax.rem(slab + 1, slabs), chan)

    def load(src, dst, sem):
        copy = pltpu.make_async_copy(src, dst, sem)
        copy.start()
        return copy

    c_grad = load(grad_center, grads.at[0], in_sem.at[0])
    r_grad = load(grad_radius, grads.at[1], in_sem.at[1])
    s_two = load(state_two, states.at[1], in_sem.at[2])

    barrier = pltpu.get_barrier_semaphore()
    for peer in (partner, sibling, above, below):
        pl.semaphore_signal(barrier, inc=1, device_id=peer, device_id_type=MESH)

    @pl.loop(1, members)
    def _(d):
        pl.semaphore_signal(
            barrier, inc=1, device_id=one_dev(lax.rem(pos_one + d, members)), device_id_type=MESH
        )

    @pl.loop(1, nz)
    def _(d):
        pl.semaphore_signal(
            barrier, inc=1, device_id=two_dev(lax.rem(pos_two + d, nz)), device_id_type=MESH
        )

    w_rows = (
        pl.ds(pl.multiple_of(chan * 128, 128), 128),
        pl.ds(pl.multiple_of((1 - chan) * 128, 128), 128),
    )

    def load_w(src, layer):
        for tap in range(9):
            for half in range(2):
                pltpu.make_async_copy(
                    src.at[tap, w_rows[half], :],
                    wcat.at[layer, pl.ds(128 * half, 128), pl.ds(128 * tap, 128)],
                    w_sem.at[layer],
                ).start()

    def wait_w(layer):
        pltpu.make_async_copy(wcat.at[layer], wcat.at[layer], w_sem.at[layer]).wait()

    load_w(weight_two, 1)
    acts = ((center_in, radius_in), (hidden_center, hidden_radius))
    act_own = [[load(acts[l][x], act.at[l, x, 0], act_sem.at[2 * l + x]) for x in range(2)] for l in range(2)]
    s_one = load(state_one, states.at[0], in_sem.at[3])
    load_w(weight_one, 0)

    c_grad.wait()
    r_grad.wait()
    s_two.wait()
    for r in range(rows):
        at = pl.ds(r * width, width)
        sc, sr = relu_back(grads[0, at, :].astype(F32), grads[1, at, :].astype(F32), states[1, at, :])
        skip[0, at, :] = sc
        skip[1, at, :] = sr

    column = lax.broadcasted_iota(jnp.int32, (width, 128), 0)

    def place(x, row, value):
        wide = value.astype(F32)
        later = jnp.where(column == width - 1, 0.0, pltpu.roll(wide, width - 1, 0)).astype(BF16)
        sooner = jnp.where(column == 0, 0.0, pltpu.roll(wide, 1, 0)).astype(BF16)
        for a in range(3):
            r = row - 2 + a
            if 0 <= r < rows:
                for b, shifted in enumerate((later, value, sooner)):
                    cols[x, pl.ds(r * width, width), pl.ds(128 * (3 * a + b), 128)] = shifted

    def place_inside(source):
        for x in range(2):
            for r in range(rows):
                place(x, r + 1, source[x, pl.ds(r * width, width), :])

    def send_halo(source, layer):
        up = pltpu.make_async_remote_copy(
            source.at[:, pl.ds(0, width), :], halo.at[layer, 1],
            halo_ss.at[layer, 0], halo_rs.at[layer, 1], device_id=above, device_id_type=MESH,
        )
        down = pltpu.make_async_remote_copy(
            source.at[:, pl.ds((rows - 1) * width, width), :], halo.at[layer, 0],
            halo_ss.at[layer, 1], halo_rs.at[layer, 0], device_id=below, device_id_type=MESH,
        )
        up.start()
        down.start()
        return up, down

    def place_halo(copies, layer):
        copies[0].wait()
        copies[1].wait()
        top = slab > 0
        bottom = slab < slabs - 1
        for x in range(2):
            above_row = halo[layer, 0, x].astype(F32)
            below_row = halo[layer, 1, x].astype(F32)
            place(x, 0, jnp.where(top, above_row, 0.0).astype(BF16))
            place(x, rows + 1, jnp.where(bottom, below_row, 0.0).astype(BF16))

    def send_act(layer):
        copies = []
        for x in range(2):
            copy = pltpu.make_async_remote_copy(
                act.at[layer, x, 0], act.at[layer, x, 1],
                act_ss.at[layer, x], act_rs.at[layer, x], device_id=partner, device_id_type=MESH,
            )
            act_own[layer][x].wait()
            copy.start()
            copies.append(copy)
        return copies

    def convolve(layer):
        copies = []
        for x in range(2):
            weight = wcat[layer] if x == 0 else wabs[layer]
            both = lax.dot_general(
                cols[x], weight, (((1,), (1,)), ((), ())), preferred_element_type=F32
            )
            part_own[x] = both[:, :128]
            part_send[layer, x] = both[:, 128:].astype(BF16)
            copy = pltpu.make_async_remote_copy(
                part_send.at[layer, x], part_recv.at[layer, x],
                part_ss.at[layer, x], part_rs.at[layer, x], device_id=partner, device_id_type=MESH,
            )
            copy.start()
            copies.append(copy)
        return copies

    def turn_own(layer):
        for x in range(2):
            act_t[x, :128, :] = act[layer, x, 0].T

    def kernel_terms(layer, copies):
        for x in range(2):
            copies[x].wait()
            act_t[x, 128:, :] = act[layer, x, 1].T
        for a in range(3):
            at = pl.ds(384 * a, 384)
            kc = jnp.dot(act_t[0], cols[0, :, at], preferred_element_type=F32)
            kr = jnp.dot(act_t[1], cols[1, :, at], preferred_element_type=F32)
            w = wcat[layer, :, at].astype(F32)
            kr = jnp.where(w > 0.0, kr, jnp.where(w < 0.0, -kr, 0.0))
            k_full[1 - layer, :, at] = scale * (kc + kr)

    place_inside(skip)
    pl.semaphore_wait(barrier, 4 + members - 1 + nz - 1)
    halo_two = send_halo(skip, 1)
    act_two = send_act(1)
    wait_w(1)
    wabs[1] = jnp.abs(wcat[1])
    turn_own(1)
    place_halo(halo_two, 1)
    part_two = convolve(1)
    act_one = send_act(0)
    kernel_terms(1, act_two)

    turn_own(0)
    wait_w(0)
    wabs[0] = jnp.abs(wcat[0])
    s_one.wait()
    for copy in part_two:
        copy.wait()
    for r in range(rows):
        at = pl.ds(r * width, width)
        back_c = part_own[0, at, :] + part_recv[1, 0, at, :].astype(F32)
        back_r = part_own[1, at, :] + part_recv[1, 1, at, :].astype(F32)
        ic, ir = relu_back(back_c, back_r, states[0, at, :])
        inner[0, at, :] = ic
        inner[1, at, :] = ir
    halo_one = send_halo(inner, 0)
    place_inside(inner)
    place_halo(halo_one, 0)
    kernel_terms(0, act_one)

    k_send[...] = k_full[1 - core].astype(BF16)
    to_core = pltpu.make_async_remote_copy(
        k_send, k_recv, core_sem.at[0], core_sem.at[1], device_id=sibling, device_id_type=MESH
    )
    to_core.start()
    part_one = convolve(0)
    to_core.wait()
    k_mine[...] = (k_full[core] + k_recv[...].astype(F32)).astype(BF16)

    def rows_of(j):
        return pl.ds(pl.multiple_of(j * chunk, chunk), chunk)

    def one_copy(d):
        j = lax.rem(pos_one + d, members)
        return pltpu.make_async_remote_copy(
            k_mine.at[rows_of(j), :], got_one.at[pos_one],
            one_ss.at[d - 1], one_rs.at[d - 1], device_id=one_dev(j), device_id_type=MESH,
        )

    @pl.loop(1, members)
    def _(d):
        one_copy(d).start()

    got_one[pos_one] = k_mine[rows_of(pos_one), :]

    outs = []
    for x, out in enumerate((out_c, out_r)):
        part_one[x].wait()
        final[x] = (
            skip[x].astype(F32) + part_own[x] + part_recv[0, x].astype(F32)
        )
        outs.append(load(final.at[x], out, out_sem.at[x]))

    @pl.loop(1, members)
    def _(d):
        one_copy(d).wait()

    total = got_one[0].astype(F32)
    for j in range(1, members):
        total = total + got_one[j].astype(F32)
    two[...] = total.astype(BF16)

    def two_copy(d):
        return pltpu.make_async_remote_copy(
            two, got_two.at[pos_two], two_ss.at[d - 1], two_rs.at[d - 1],
            device_id=two_dev(lax.rem(pos_two + d, nz)), device_id_type=MESH,
        )

    @pl.loop(1, nz)
    def _(d):
        two_copy(d).start()

    got_two[pos_two] = two[...]

    @pl.loop(1, nz)
    def _(d):
        two_copy(d).wait()

    total = got_two[0].astype(F32)
    for j in range(1, nz):
        total = total + got_two[j].astype(F32)
    result[core, rows_of(pos_one), :] = total.astype(BF16)

    def back_copy(d):
        j = lax.rem(pos_one + d, members)
        mine = result.at[core, rows_of(pos_one), :]
        return pltpu.make_async_remote_copy(
            mine, mine, back_ss.at[d - 1], back_rs.at[d - 1], device_id=one_dev(j), device_id_type=MESH
        )

    def fwd_copy(d):
        there = result.at[core, rows_of(lax.rem(pos_one - d + members, members)), :]
        return pltpu.make_async_remote_copy(
            there, there, fwd_ss.at[d], fwd_rs.at[d], device_id=sibling, device_id_type=MESH
        )

    def back_wait(d):
        there = result.at[core, rows_of(lax.rem(pos_one - d + members, members)), :]
        return pltpu.make_async_remote_copy(
            there, there, back_ss.at[d - 1], back_rs.at[d - 1], device_id=sibling, device_id_type=MESH
        )

    @pl.loop(1, members)
    def _(d):
        back_copy(d).start()

    fwd_copy(0).start()

    @pl.loop(1, members)
    def _(d):
        back_wait(d).wait_recv()
        fwd_copy(d).start()

    @pl.loop(1, members)
    def _(d):
        back_copy(d).wait_send()

    @pl.loop(0, members)
    def _(d):
        fwd_copy(d).wait_send()

    @pl.loop(0, members)
    def _(d):
        there = result.at[1 - core, pl.ds(0, chunk), :]
        pltpu.make_async_remote_copy(
            there, there, fwd_ss.at[d], fwd_rs.at[d], device_id=sibling, device_id_type=MESH
        ).wait_recv()

    k_outs = []
    for k in range(2):
        for half in range(2):
            k_outs.append(
                load(
                    result.at[k, pl.ds(128 * half, 128), :],
                    out_k.at[k, w_rows[half], :],
                    k_out_sem.at[k, half],
                )
            )
    for copy in outs + k_outs:
        copy.wait()


def body(sizes, *arrays):
    ny, nz, rows, width, _ = sizes
    pix = rows * width
    flat = [a.reshape(pix, 128) for a in arrays[:6]]
    weights = [w.reshape(9, 256, 128) for w in arrays[6:8]]
    grads = [a.reshape(pix, 128) for a in arrays[8:]]
    members = 2 * ny
    chunk = 256 // members
    dma = pltpu.SemaphoreType.DMA
    out_c, out_r, out_k = pl.pallas_call(
        functools.partial(kernel, sizes),
        name="interval_back",
        out_shape=(
            jax.ShapeDtypeStruct((pix, 128), F32),
            jax.ShapeDtypeStruct((pix, 128), F32),
            jax.ShapeDtypeStruct((2, 256, 1152), BF16),
        ),
        in_specs=[pl.BlockSpec(memory_space=pl.ANY)] * 10,
        out_specs=(pl.BlockSpec(memory_space=pl.ANY),) * 3,
        scratch_shapes=[
            pltpu.VMEM((2, pix, 128), BF16),
            pltpu.VMEM((2, pix, 128), jnp.int32),
            pltpu.VMEM((2, 256, 1152), BF16),
            pltpu.VMEM((2, 256, 1152), BF16),
            pltpu.VMEM((2, 2, 2, pix, 128), BF16),
            pltpu.VMEM((2, 256, pix), BF16),
            pltpu.VMEM((2, pix, 128), BF16),
            pltpu.VMEM((2, pix, 128), BF16),
            pltpu.VMEM((2, 2, 2, width, 128), BF16),
            pltpu.VMEM((2, pix, 1152), BF16),
            pltpu.VMEM((2, pix, 128), F32),
            pltpu.VMEM((2, 2, pix, 128), BF16),
            pltpu.VMEM((2, 2, pix, 128), BF16),
            pltpu.VMEM((2, pix, 128), F32),
            pltpu.VMEM((2, 256, 1152), F32),
            pltpu.VMEM((256, 1152), BF16),
            pltpu.VMEM((256, 1152), BF16),
            pltpu.VMEM((256, 1152), BF16),
            pltpu.VMEM((members, chunk, 1152), BF16),
            pltpu.VMEM((chunk, 1152), BF16),
            pltpu.VMEM((nz, chunk, 1152), BF16),
            pltpu.VMEM((2, 256, 1152), BF16),
            dma((4,)),
            dma((2,)),
            dma((4,)),
            dma((2, 2)),
            dma((2, 2)),
            dma((2, 2)),
            dma((2, 2)),
            dma((2, 2)),
            dma((2, 2)),
            dma((2,)),
            dma((members - 1,)),
            dma((members - 1,)),
            dma((nz - 1,)),
            dma((nz - 1,)),
            dma((members - 1,)),
            dma((members - 1,)),
            dma((members,)),
            dma((members,)),
            dma((2,)),
            dma((2, 2)),
        ],
        compiler_params=pltpu.CompilerParams(
            collective_id=0, has_side_effects=True, vmem_limit_bytes=48 << 20
        ),
    )(*flat, *weights, *grads)
    kernels = out_k.reshape(2, 256, 9, 128).transpose(0, 2, 1, 3).reshape(2, 3, 3, 256, 128)
    shape = arrays[0].shape
    return out_c.reshape(shape), out_r.reshape(shape), kernels[1], kernels[0]


def solution(mesh):
    wide = P("dp", "slab", None, "chan")
    narrow = P(None, None, None, "chan")
    ny, nz = mesh.shape["dp"] // 2, mesh.shape["slab"] // 2

    def whole(*arrays):
        images, height, width, _ = arrays[0].shape
        sizes = (ny, nz, height // (2 * nz), width, 1.0 / math.sqrt(images * height * width))
        return jax.shard_map(
            functools.partial(body, sizes),
            mesh=mesh,
            in_specs=(wide,) * 6 + (narrow,) * 2 + (wide,) * 2,
            out_specs=(wide, wide, narrow, narrow),
            check_vma=False,
        )(*arrays)

    return whole
```

time: 1290 us -> 91.9 us (0.07); the launches traced: 1270 us -> 91.5 us
  blocking collectives: 1130 us -> 0 us
  Pallas kernels: 0 us -> 77.2 us
  waiting for transfers between devices: 45.9 us -> 0 us
  matrix products: 38.9 us -> 0 us
  other arithmetic: 14.2 us -> 0 us
  between operations: 14.3 us -> 0.68 us
    psum x1 -> x0, blocking collectives: 1100 us -> none  [total_over(): return lax.psum(values, ('dp', 'slab'))]
    pallas_call x0 -> x1, Pallas kernels: none -> 77.2 us  [body(): pl.pallas_call(functools.partial(kernel, sizes), name='interval_back', ou...]
    reduce_scatter x4 -> x0, waiting for transfers between devices: 43 us -> none  [the longest x2 27 us: layer_back(): lax.psum_scatter(back_c, 'chan', scatter_dimension=3, tiled=True)]
    dot_general x72 -> x0, matrix products: 38.9 us -> none  [the longest x18 10.7 us: layer_back(): jnp.einsum('bhwi,bhwo->io', act_c, window[0], preferred_element_type=jnp....]
    all_gather x4 -> x0, blocking collectives: 26.4 us -> none  [the longest x1 7.62 us: body(): lax.all_gather(hidden_radius, 'chan', axis=3, tiled=True)]
  transfers between devices with their start and end apart: 8 -> 0, of which waited for: 3 -> 0; matrix products, arithmetic and copies ran while one was open for 2% -> 0% of each run, Pallas kernels for 0% -> 0%
where the time goes in v1:
time: 91.9 us; the launch traced here: 91.5 us
  Pallas kernels  77.2 us (84%)
  local copies, waits for them, and re-layouts  13.7 us (15%)
    pallas_call x1, Pallas kernels, body(): pl.pallas_call(functools.partial(kernel, sizes), name='interval_back', ou...  77.2 us
    unnamed x24, local copies, waits for them, and re-layouts  13 us

profile of v1, /device:TPU:1, one launch (start us, length us, event | category | flops | bytes accessed | tf_op | source)
XLA Modules:
  0.0 91.5 jit_solution(3995603665226021476)
XLA Ops:
  0.6 0.0 copy-start
  0.6 1.1 %copy-done = bf16[3,3,256,128]{3,2,1,0:T(8,128)(2,1)S(1)} copy-done((bf16[3,3,256,128]{3,2,1,0:T(8,128)(2,1)S(1)}, bf16[3,3,256,128]{3,2,1,0:T(8,128)(2,1)}, u32[]{:S(2)}) %copy-start) | copy-done | bytes 589848
  1.7 0.0 copy-start.1
  1.7 1.1 %copy-done.1 = bf16[3,3,256,128]{3,2,1,0:T(8,128)(2,1)S(1)} copy-done((bf16[3,3,256,128]{3,2,1,0:T(8,128)(2,1)S(1)}, bf16[3,3,256,128]{3,2,1,0:T(8,128)(2,1)}, u32[]{:S(2)}) %copy-start.1) | copy-done | bytes 589848
  2.8 0.0 copy-start.2
  2.8 0.9 %copy-done.2 = s32[1,4,128,128]{3,2,1,0:T(8,128)S(1)} copy-done((s32[1,4,128,128]{3,2,1,0:T(8,128)S(1)}, s32[1,4,128,128]{3,2,1,0:T(8,128)}, u32[]{:S(2)}) %copy-start.2) | copy-done | bytes 262168
  3.7 0.0 copy-start.3
  3.7 0.9 %copy-done.3 = s32[1,4,128,128]{3,2,1,0:T(8,128)S(1)} copy-done((s32[1,4,128,128]{3,2,1,0:T(8,128)S(1)}, s32[1,4,128,128]{3,2,1,0:T(8,128)}, u32[]{:S(2)}) %copy-start.3) | copy-done | bytes 262168
  4.7 0.0 copy-start.4
  4.7 0.9 copy-done.4
  5.6 0.0 copy-start.5
  5.6 0.9 copy-done.5
  6.5 0.0 copy-start.6
  6.5 0.9 copy-done.6
  7.4 0.0 copy-start.7
  7.4 0.9 copy-done.7
  8.3 0.0 copy-start.8
  8.3 0.9 copy-done.8
  9.2 0.0 copy-start.9
  9.2 0.9 copy-done.9
  10.1 77.2 %interval_back.1 = (f32[512,128]{1,0:T(8,128)S(1)}, f32[512,128]{1,0:T(8,128)S(1)}, bf16[2,256,1152]{2,1,0:T(8,128)(2,1)S(1)}) custom-call(bf16[512,128]{1,0:T(8,128)(2,1)S(1)} %bitcast.23, bf16[512,128]{1,0:T(8,128)(2,1)S(1)} %bitcast.24, bf16[512,128]{1,0:T(8,128)(2,1)S(1)} %bitcast.25, bf16[512,128]{1,0:T(8,128)(2,1)S(1)} %bitcast.26, ...), custom_call_target="tpu_custom_call" | custom-call | tf_op jit(solution)/shard_map/interval_back/pallas_call | solution.py:413
  87.3 0.6 copy.16
  87.9 0.1 fusion
  88.0 1.1 %copy.18 = bf16[3,3,256,128]{3,2,1,0:T(8,128)(2,1)} copy(bf16[3,3,256,128]{2,3,1,0:T(8,128)(2,1)S(1)} %bitcast.31) | data formatting | bytes 1179648
  89.1 1.1 %copy.17 = bf16[3,3,256,128]{3,2,1,0:T(8,128)(2,1)} copy(bf16[3,3,256,128]{2,3,1,0:T(8,128)(2,1)S(1)} %bitcast.30) | data formatting | bytes 1179648
  90.1 0.7 copy.21
  90.8 0.7 copy.22
Async XLA Ops:
  0.6 1.1 %copy-start = (bf16[3,3,256,128]{3,2,1,0:T(8,128)(2,1)S(1)}, bf16[3,3,256,128]{3,2,1,0:T(8,128)(2,1)}, u32[]{:S(2)}) copy-start(bf16[3,3,256,128]{3,2,1,0:T(8,128)(2,1)} %param.16) | copy-start | bytes 1769476
  1.7 1.1 %copy-start.1 = (bf16[3,3,256,128]{3,2,1,0:T(8,128)(2,1)S(1)}, bf16[3,3,256,128]{3,2,1,0:T(8,128)(2,1)}, u32[]{:S(2)}) copy-start(bf16[3,3,256,128]{3,2,1,0:T(8,128)(2,1)} %param.17) | copy-start | bytes 1769476
  2.8 0.9 %copy-start.2 = (s32[1,4,128,128]{3,2,1,0:T(8,128)S(1)}, s32[1,4,128,128]{3,2,1,0:T(8,128)}, u32[]{:S(2)}) copy-start(s32[1,4,128,128]{3,2,1,0:T(8,128)} %param.14) | copy-start | bytes 786436
  3.7 0.9 %copy-start.3 = (s32[1,4,128,128]{3,2,1,0:T(8,128)S(1)}, s32[1,4,128,128]{3,2,1,0:T(8,128)}, u32[]{:S(2)}) copy-start(s32[1,4,128,128]{3,2,1,0:T(8,128)} %param.15) | copy-start | bytes 786436
  4.7 0.9 copy-start.4
  5.6 0.9 copy-start.5
  6.5 0.9 copy-start.6
  7.4 0.9 copy-start.7
  8.3 0.9 copy-start.8
  9.2 0.9 copy-start.9

commit v2 on v1

--- a/solution.py
+++ b/solution.py
@@ -50,7 +50,6 @@
     part_recv,
     final,
     k_full,
-    k_send,
     k_recv,
     k_mine,
     got_one,
@@ -66,7 +65,8 @@
     act_rs,
     part_ss,
     part_rs,
-    core_sem,
+    core_ss,
+    core_rs,
     one_ss,
     one_rs,
     two_ss,
@@ -247,7 +247,140 @@
             kr = jnp.dot(act_t[1], cols[1, :, at], preferred_element_type=F32)
             w = wcat[layer, :, at].astype(F32)
             kr = jnp.where(w > 0.0, kr, jnp.where(w < 0.0, -kr, 0.0))
-            k_full[1 - layer, :, at] = scale * (kc + kr)
+            k_full[layer, :, at] = scale * (kc + kr)
+
+    def own_cols(which):
+        return pl.ds(pl.multiple_of(which * 512, 512), 640)
+
+    def rows_of(j):
+        return pl.ds(pl.multiple_of(j * chunk, chunk), chunk)
+
+    def far_first(i, count):
+        k = lax.div(i + 1, 2)
+        return count // 2 + jnp.where(lax.rem(i, 2) == 1, k, -k)
+
+    def core_copy(layer):
+        return pltpu.make_async_remote_copy(
+            k_full.at[layer, :, own_cols(1 - core)], k_recv.at[layer],
+            core_ss.at[layer], core_rs.at[layer], device_id=sibling, device_id_type=MESH,
+        )
+
+    def one_copy(layer, d):
+        j = lax.rem(pos_one + d, members)
+        return pltpu.make_async_remote_copy(
+            k_mine.at[layer, rows_of(j), :], got_one.at[layer, pos_one],
+            one_ss.at[layer, d - 1], one_rs.at[layer, d - 1],
+            device_id=one_dev(j), device_id_type=MESH,
+        )
+
+    def two_copy(layer, d):
+        return pltpu.make_async_remote_copy(
+            two.at[layer], got_two.at[layer, pos_two],
+            two_ss.at[layer, d - 1], two_rs.at[layer, d - 1],
+            device_id=two_dev(lax.rem(pos_two + d, nz)), device_id_type=MESH,
+        )
+
+    def back_copy(layer, d):
+        j = lax.rem(pos_one + d, members)
+        mine = result.at[layer, core, rows_of(pos_one), :]
+        return pltpu.make_async_remote_copy(
+            mine, mine, back_ss.at[layer, d - 1], back_rs.at[layer, d - 1],
+            device_id=one_dev(j), device_id_type=MESH,
+        )
+
+    def back_from(layer, d):
+        there = result.at[layer, core, rows_of(lax.rem(pos_one - d + members, members)), :]
+        return pltpu.make_async_remote_copy(
+            there, there, back_ss.at[layer, d - 1], back_rs.at[layer, d - 1],
+            device_id=sibling, device_id_type=MESH,
+        )
+
+    def fwd_copy(layer, d):
+        there = result.at[layer, core, rows_of(lax.rem(pos_one - d + members, members)), :]
+        return pltpu.make_async_remote_copy(
+            there, there, fwd_ss.at[layer, d], fwd_rs.at[layer, d],
+            device_id=sibling, device_id_type=MESH,
+        )
+
+    def fwd_from(layer, d):
+        there = result.at[layer, 1 - core, pl.ds(0, chunk), :]
+        return pltpu.make_async_remote_copy(
+            there, there, fwd_ss.at[layer, d], fwd_rs.at[layer, d],
+            device_id=sibling, device_id_type=MESH,
+        )
+
+    def scatter(layer):
+        core_copy(layer).wait()
+        own = k_full[layer, :, own_cols(core)]
+        k_mine[layer] = (own + k_recv[layer]).astype(BF16)
+
+        @pl.loop(0, members - 1)
+        def _(i):
+            one_copy(layer, far_first(i, members)).start()
+
+        got_one[layer, pos_one] = k_mine[layer, rows_of(pos_one), :]
+
+    def spread(layer):
+        @pl.loop(1, members)
+        def _(d):
+            one_copy(layer, d).wait()
+
+        total = got_one[layer, 0].astype(F32)
+        for j in range(1, members):
+            total = total + got_one[layer, j].astype(F32)
+        two[layer] = total.astype(BF16)
+
+        @pl.loop(0, nz - 1)
+        def _(i):
+            two_copy(layer, far_first(i, nz)).start()
+
+        got_two[layer, pos_two] = two[layer]
+
+    def gather(layer):
+        @pl.loop(1, nz)
+        def _(d):
+            two_copy(layer, d).wait()
+
+        total = got_two[layer, 0].astype(F32)
+        for j in range(1, nz):
+            total = total + got_two[layer, j].astype(F32)
+        result[layer, core, rows_of(pos_one), :] = total.astype(BF16)
+
+        @pl.loop(0, members - 1)
+        def _(i):
+            back_copy(layer, far_first(i, members)).start()
+
+        fwd_copy(layer, 0).start()
+
+    def write_out(layer, which):
+        for tap in range(0, 5) if which == 0 else range(5, 9):
+            for half in range(2):
+                pltpu.make_async_copy(
+                    result.at[layer, which, pl.ds(128 * half, 128), pl.ds(128 * (tap - 4 * which), 128)],
+                    out_k.at[layer, tap, w_rows[half], :],
+                    k_out_sem.at[layer],
+                ).start()
+
+    def deliver(layer):
+        @pl.loop(1, members)
+        def _(d):
+            back_from(layer, d).wait_recv()
+            fwd_copy(layer, d).start()
+
+        @pl.loop(0, members)
+        def _(d):
+            fwd_from(layer, d).wait_recv()
+
+        write_out(layer, 0)
+        write_out(layer, 1)
+
+        @pl.loop(1, members)
+        def _(d):
+            back_copy(layer, d).wait_send()
+
+        @pl.loop(0, members)
+        def _(d):
+            fwd_copy(layer, d).wait_send()
 
     place_inside(skip)
     pl.semaphore_wait(barrier, 4 + members - 1 + nz - 1)
@@ -259,12 +392,15 @@
     place_halo(halo_two, 1)
     part_two = convolve(1)
     act_one = send_act(0)
+
     kernel_terms(1, act_two)
-
+    core_copy(1).start()
     turn_own(0)
     wait_w(0)
     wabs[0] = jnp.abs(wcat[0])
     s_one.wait()
+    scatter(1)
+
     for copy in part_two:
         copy.wait()
     for r in range(rows):
@@ -277,127 +413,44 @@
     halo_one = send_halo(inner, 0)
     place_inside(inner)
     place_halo(halo_one, 0)
+
     kernel_terms(0, act_one)
-
-    k_send[...] = k_full[1 - core].astype(BF16)
-    to_core = pltpu.make_async_remote_copy(
-        k_send, k_recv, core_sem.at[0], core_sem.at[1], device_id=sibling, device_id_type=MESH
-    )
-    to_core.start()
+    core_copy(0).start()
+    spread(1)
+    scatter(0)
     part_one = convolve(0)
-    to_core.wait()
-    k_mine[...] = (k_full[core] + k_recv[...].astype(F32)).astype(BF16)
-
-    def rows_of(j):
-        return pl.ds(pl.multiple_of(j * chunk, chunk), chunk)
-
-    def one_copy(d):
-        j = lax.rem(pos_one + d, members)
-        return pltpu.make_async_remote_copy(
-            k_mine.at[rows_of(j), :], got_one.at[pos_one],
-            one_ss.at[d - 1], one_rs.at[d - 1], device_id=one_dev(j), device_id_type=MESH,
-        )
-
-    @pl.loop(1, members)
-    def _(d):
-        one_copy(d).start()
-
-    got_one[pos_one] = k_mine[rows_of(pos_one), :]
+    gather(1)
+    spread(0)
 
     outs = []
     for x, out in enumerate((out_c, out_r)):
         part_one[x].wait()
-        final[x] = (
-            skip[x].astype(F32) + part_own[x] + part_recv[0, x].astype(F32)
-        )
+        final[x] = skip[x].astype(F32) + part_own[x] + part_recv[0, x].astype(F32)
         outs.append(load(final.at[x], out, out_sem.at[x]))
-
-    @pl.loop(1, members)
-    def _(d):
-        one_copy(d).wait()
-
-    total = got_one[0].astype(F32)
-    for j in range(1, members):
-        total = total + got_one[j].astype(F32)
-    two[...] = total.astype(BF16)
-
-    def two_copy(d):
-        return pltpu.make_async_remote_copy(
-            two, got_two.at[pos_two], two_ss.at[d - 1], two_rs.at[d - 1],
-            device_id=two_dev(lax.rem(pos_two + d, nz)), device_id_type=MESH,
-        )
-
-    @pl.loop(1, nz)
-    def _(d):
-        two_copy(d).start()
-
-    got_two[pos_two] = two[...]
-
-    @pl.loop(1, nz)
-    def _(d):
-        two_copy(d).wait()
-
-    total = got_two[0].astype(F32)
-    for j in range(1, nz):
-        total = total + got_two[j].astype(F32)
-    result[core, rows_of(pos_one), :] = total.astype(BF16)
-
-    def back_copy(d):
-        j = lax.rem(pos_one + d, members)
-        mine = result.at[core, rows_of(pos_one), :]
-        return pltpu.make_async_remote_copy(
-            mine, mine, back_ss.at[d - 1], back_rs.at[d - 1], device_id=one_dev(j), device_id_type=MESH
-        )
-
-    def fwd_copy(d):
-        there = result.at[core, rows_of(lax.rem(pos_one - d + members, members)), :]
-        return pltpu.make_async_remote_copy(
-            there, there, fwd_ss.at[d], fwd_rs.at[d], device_id=sibling, device_id_type=MESH
-        )
-
-    def back_wait(d):
-        there = result.at[core, rows_of(lax.rem(pos_one - d + members, members)), :]
-        return pltpu.make_async_remote_copy(
-            there, there, back_ss.at[d - 1], back_rs.at[d - 1], device_id=sibling, device_id_type=MESH
-        )
-
-    @pl.loop(1, members)
-    def _(d):
-        back_copy(d).start()
-
-    fwd_copy(0).start()
-
-    @pl.loop(1, members)
-    def _(d):
-        back_wait(d).wait_recv()
-        fwd_copy(d).start()
-
-    @pl.loop(1, members)
-    def _(d):
-        back_copy(d).wait_send()
-
-    @pl.loop(0, members)
-    def _(d):
-        fwd_copy(d).wait_send()
-
-    @pl.loop(0, members)
-    def _(d):
-        there = result.at[1 - core, pl.ds(0, chunk), :]
-        pltpu.make_async_remote_copy(
-            there, there, fwd_ss.at[d], fwd_rs.at[d], device_id=sibling, device_id_type=MESH
-        ).wait_recv()
-
-    k_outs = []
-    for k in range(2):
-        for half in range(2):
-            k_outs.append(
-                load(
-                    result.at[k, pl.ds(128 * half, 128), :],
-                    out_k.at[k, w_rows[half], :],
-                    k_out_sem.at[k, half],
-                )
-            )
-    for copy in outs + k_outs:
+    deliver(1)
+    gather(0)
+    deliver(0)
+    for copy in outs:
+        copy.wait()
+    for layer in range(2):
+        pltpu.make_async_copy(out_k.at[layer], out_k.at[layer], k_out_sem.at[layer]).wait()
+
+
+def hand_over(made_c, made_r, made_k, out_c, out_r, out_one, out_two, wide, taps, load_sem, sem):
+    sources = (made_c, made_r, made_k.at[0], made_k.at[1])
+    buffers = (wide.at[0], wide.at[1], taps.at[0], taps.at[1])
+    targets = (out_c, out_r, out_one, out_two)
+    loads = []
+    stores = []
+    for i in range(4):
+        loads.append(pltpu.make_async_copy(sources[i], buffers[i], load_sem.at[i]))
+        stores.append(pltpu.make_async_copy(buffers[i], targets[i], sem.at[i]))
+    for copy in loads:
+        copy.start()
+    for i in range(4):
+        loads[i].wait()
+        stores[i].start()
+    for copy in stores:
         copy.wait()
 
 
@@ -416,7 +469,7 @@
         out_shape=(
             jax.ShapeDtypeStruct((pix, 128), F32),
             jax.ShapeDtypeStruct((pix, 128), F32),
-            jax.ShapeDtypeStruct((2, 256, 1152), BF16),
+            jax.ShapeDtypeStruct((2, 9, 256, 128), BF16),
         ),
         in_specs=[pl.BlockSpec(memory_space=pl.ANY)] * 10,
         out_specs=(pl.BlockSpec(memory_space=pl.ANY),) * 3,
@@ -436,13 +489,12 @@
             pltpu.VMEM((2, 2, pix, 128), BF16),
             pltpu.VMEM((2, pix, 128), F32),
             pltpu.VMEM((2, 256, 1152), F32),
-            pltpu.VMEM((256, 1152), BF16),
-            pltpu.VMEM((256, 1152), BF16),
-            pltpu.VMEM((256, 1152), BF16),
-            pltpu.VMEM((members, chunk, 1152), BF16),
-            pltpu.VMEM((chunk, 1152), BF16),
-            pltpu.VMEM((nz, chunk, 1152), BF16),
-            pltpu.VMEM((2, 256, 1152), BF16),
+            pltpu.VMEM((2, 256, 640), F32),
+            pltpu.VMEM((2, 256, 640), BF16),
+            pltpu.VMEM((2, members, chunk, 640), BF16),
+            pltpu.VMEM((2, chunk, 640), BF16),
+            pltpu.VMEM((2, nz, chunk, 640), BF16),
+            pltpu.VMEM((2, 2, 256, 640), BF16),
             dma((4,)),
             dma((2,)),
             dma((4,)),
@@ -453,24 +505,44 @@
             dma((2, 2)),
             dma((2, 2)),
             dma((2,)),
-            dma((members - 1,)),
-            dma((members - 1,)),
-            dma((nz - 1,)),
-            dma((nz - 1,)),
-            dma((members - 1,)),
-            dma((members - 1,)),
-            dma((members,)),
-            dma((members,)),
             dma((2,)),
-            dma((2, 2)),
+            dma((2, members - 1)),
+            dma((2, members - 1)),
+            dma((2, nz - 1)),
+            dma((2, nz - 1)),
+            dma((2, members - 1)),
+            dma((2, members - 1)),
+            dma((2, members)),
+            dma((2, members)),
+            dma((2,)),
+            dma((2,)),
         ],
         compiler_params=pltpu.CompilerParams(
-            collective_id=0, has_side_effects=True, vmem_limit_bytes=48 << 20
+            collective_id=0, has_side_effects=True, vmem_limit_bytes=62 << 20
         ),
     )(*flat, *weights, *grads)
-    kernels = out_k.reshape(2, 256, 9, 128).transpose(0, 2, 1, 3).reshape(2, 3, 3, 256, 128)
     shape = arrays[0].shape
-    return out_c.reshape(shape), out_r.reshape(shape), kernels[1], kernels[0]
+    out_c, out_r, k_one, k_two = pl.pallas_call(
+        hand_over,
+        name="hand_over",
+        out_shape=(
+            jax.ShapeDtypeStruct((pix, 128), F32),
+            jax.ShapeDtypeStruct((pix, 128), F32),
+            jax.ShapeDtypeStruct((9, 256, 128), BF16),
+            jax.ShapeDtypeStruct((9, 256, 128), BF16),
+        ),
+        in_specs=[pl.BlockSpec(memory_space=pl.ANY)] * 3,
+        out_specs=(pl.BlockSpec(memory_space=pl.ANY),) * 4,
+        scratch_shapes=[
+            pltpu.VMEM((2, pix, 128), F32),
+            pltpu.VMEM((2, 9, 256, 128), BF16),
+            dma((4,)),
+            dma((4,)),
+        ],
+        compiler_params=pltpu.CompilerParams(vmem_limit_bytes=62 << 20),
+    )(out_c, out_r, out_k)
+    taps = (3, 3, 256, 128)
+    return out_c.reshape(shape), out_r.reshape(shape), k_one.reshape(taps), k_two.reshape(taps)
 
 
 def solution(mesh):

time: 91.9 us -> 77 us (0.84)
  local copies, waits for them, and re-layouts: 13.7 us -> 0 us
  Pallas kernels: 77.2 us -> 76.2 us
    unnamed x24 -> x0, local copies, waits for them, and re-layouts: 13 us -> none
    pallas_call x1, Pallas kernels: 77.2 us -> 73.9 us  [body(): pl.pallas_call(functools.partial(kernel, sizes), name='interval_back', ou...]
    pallas_call x0 -> x1, Pallas kernels: none -> 2.3 us  [body(): pl.pallas_call(hand_over, name='hand_over', out_shape=(jax.ShapeDtypeStru...]
where the time goes in v2:
time: 77 us; the launch traced here: 76.8 us
  Pallas kernels  76.2 us (99%)
    pallas_call x1, Pallas kernels, body(): pl.pallas_call(functools.partial(kernel, sizes), name='interval_back', ou...  73.9 us
    pallas_call x1, Pallas kernels, body(): pl.pallas_call(hand_over, name='hand_over', out_shape=(jax.ShapeDtypeStru...  2.3 us

profile of v2, /device:TPU:1, one launch (start us, length us, event | category | flops | bytes accessed | tf_op | source)
XLA Modules:
  0.0 76.8 jit_solution(1920945890769186156)
XLA Ops:
  0.6 73.9 %interval_back.1 = (f32[512,128]{1,0:T(8,128)}, f32[512,128]{1,0:T(8,128)}, bf16[2,9,256,128]{3,2,1,0:T(8,128)(2,1)}) custom-call(bf16[512,128]{1,0:T(8,128)(2,1)} %bitcast.18, bf16[512,128]{1,0:T(8,128)(2,1)} %bitcast.19, bf16[512,128]{1,0:T(8,128)(2,1)} %bitcast.20, bf16[512,128]{1,0:T(8,128)(2,1)} %bitcast.21, s32[512,128]{1,0:T(8,128)} %bitcast.16, ...), custom_call_target="tpu_custom_call" | custom-call | tf_op jit(solution)/shard_map/interval_back/pallas_call | solution.py:466
  74.5 2.3 %hand_over.1 = (f32[512,128]{1,0:T(8,128)}, f32[512,128]{1,0:T(8,128)}, bf16[9,256,128]{2,1,0:T(8,128)(2,1)}, bf16[9,256,128]{2,1,0:T(8,128)(2,1)}) custom-call(f32[512,128]{1,0:T(8,128)} %get-tuple-element.11.made_c, f32[512,128]{1,0:T(8,128)} %get-tuple-element.12.made_r, bf16[2,9,256,128]{3,2,1,0:T(8,128)(2,1)} %get-tuple-element.13.made_k), custom_call_target="tpu_custom_call" | custom-call | tf_op jit(solution)/shard_map/hand_over/pallas_call | solution.py:525

commit v3 on v2

--- a/solution.py
+++ b/solution.py
@@ -91,12 +91,8 @@
     pos_two = jnp.where(first, z, y)
 
     def one_dev(j):
-        a = lax.div(j, 2)
-        return (
-            jnp.where(first, a, y) * 2 + core,
-            jnp.where(first, z, a) * 2 + lax.rem(j, 2),
-            chan,
-        )
+        a, x = lax.div(j, 2), lax.rem(j, 2)
+        return (jnp.where(first, a, y) * 2 + core, jnp.where(first, z, a) * 2 + x, chan)
 
     def two_dev(j):
         return (jnp.where(first, y, j) * 2 + core, jnp.where(first, j, z) * 2 + x_lo, chan)
@@ -115,49 +111,47 @@
     r_grad = load(grad_radius, grads.at[1], in_sem.at[1])
     s_two = load(state_two, states.at[1], in_sem.at[2])
 
+    def far_first(i, count):
+        k = lax.div(i + 1, 2)
+        return count // 2 + jnp.where(lax.rem(i, 2) == 1, k, -k)
+
     barrier = pltpu.get_barrier_semaphore()
-    for peer in (partner, sibling, above, below):
+
+    @pl.loop(0, members - 1)
+    def _(i):
+        d = far_first(i, members)
+        peer = one_dev(lax.rem(pos_one + d, members))
         pl.semaphore_signal(barrier, inc=1, device_id=peer, device_id_type=MESH)
 
-    @pl.loop(1, members)
-    def _(d):
-        pl.semaphore_signal(
-            barrier, inc=1, device_id=one_dev(lax.rem(pos_one + d, members)), device_id_type=MESH
-        )
-
-    @pl.loop(1, nz)
-    def _(d):
-        pl.semaphore_signal(
-            barrier, inc=1, device_id=two_dev(lax.rem(pos_two + d, nz)), device_id_type=MESH
-        )
-
-    w_rows = (
-        pl.ds(pl.multiple_of(chan * 128, 128), 128),
-        pl.ds(pl.multiple_of((1 - chan) * 128, 128), 128),
-    )
+    @pl.loop(0, nz - 1)
+    def _(i):
+        peer = two_dev(lax.rem(pos_two + far_first(i, nz), nz))
+        pl.semaphore_signal(barrier, inc=1, device_id=peer, device_id_type=MESH)
+
+    for peer in (partner, above, below, sibling):
+        pl.semaphore_signal(barrier, inc=1, device_id=peer, device_id_type=MESH)
+
+    own_at = pl.ds(pl.multiple_of(chan * 128, 128), 128)
+    other_at = pl.ds(pl.multiple_of((1 - chan) * 128, 128), 128)
+    lower = chan == 0
 
     def load_w(src, layer):
         for tap in range(9):
-            for half in range(2):
-                pltpu.make_async_copy(
-                    src.at[tap, w_rows[half], :],
-                    wcat.at[layer, pl.ds(128 * half, 128), pl.ds(128 * tap, 128)],
-                    w_sem.at[layer],
-                ).start()
+            pltpu.make_async_copy(
+                src.at[tap], wcat.at[layer, :, pl.ds(128 * tap, 128)], w_sem.at[layer]
+            ).start()
 
     def wait_w(layer):
         pltpu.make_async_copy(wcat.at[layer], wcat.at[layer], w_sem.at[layer]).wait()
 
-    load_w(weight_two, 1)
     acts = ((center_in, radius_in), (hidden_center, hidden_radius))
     act_own = [[load(acts[l][x], act.at[l, x, 0], act_sem.at[2 * l + x]) for x in range(2)] for l in range(2)]
     s_one = load(state_one, states.at[0], in_sem.at[3])
-    load_w(weight_one, 0)
 
     c_grad.wait()
     r_grad.wait()
     s_two.wait()
-    for r in range(rows):
+    for r in (0, rows - 1, *range(1, rows - 1)):
         at = pl.ds(r * width, width)
         sc, sr = relu_back(grads[0, at, :].astype(F32), grads[1, at, :].astype(F32), states[1, at, :])
         skip[0, at, :] = sc
@@ -165,7 +159,7 @@
 
     column = lax.broadcasted_iota(jnp.int32, (width, 128), 0)
 
-    def place(x, row, value):
+    def place(layer, x, row, value):
         wide = value.astype(F32)
         later = jnp.where(column == width - 1, 0.0, pltpu.roll(wide, width - 1, 0)).astype(BF16)
         sooner = jnp.where(column == 0, 0.0, pltpu.roll(wide, 1, 0)).astype(BF16)
@@ -173,12 +167,12 @@
             r = row - 2 + a
             if 0 <= r < rows:
                 for b, shifted in enumerate((later, value, sooner)):
-                    cols[x, pl.ds(r * width, width), pl.ds(128 * (3 * a + b), 128)] = shifted
-
-    def place_inside(source):
+                    cols[layer, x, pl.ds(r * width, width), pl.ds(128 * (3 * a + b), 128)] = shifted
+
+    def place_inside(source, layer):
         for x in range(2):
             for r in range(rows):
-                place(x, r + 1, source[x, pl.ds(r * width, width), :])
+                place(layer, x, r + 1, source[x, pl.ds(r * width, width), :])
 
     def send_halo(source, layer):
         up = pltpu.make_async_remote_copy(
@@ -201,53 +195,54 @@
         for x in range(2):
             above_row = halo[layer, 0, x].astype(F32)
             below_row = halo[layer, 1, x].astype(F32)
-            place(x, 0, jnp.where(top, above_row, 0.0).astype(BF16))
-            place(x, rows + 1, jnp.where(bottom, below_row, 0.0).astype(BF16))
-
-    def send_act(layer):
-        copies = []
-        for x in range(2):
-            copy = pltpu.make_async_remote_copy(
-                act.at[layer, x, 0], act.at[layer, x, 1],
-                act_ss.at[layer, x], act_rs.at[layer, x], device_id=partner, device_id_type=MESH,
-            )
-            act_own[layer][x].wait()
-            copy.start()
-            copies.append(copy)
-        return copies
+            place(layer, x, 0, jnp.where(top, above_row, 0.0).astype(BF16))
+            place(layer, x, rows + 1, jnp.where(bottom, below_row, 0.0).astype(BF16))
+
+    def send_act(layer, x):
+        copy = pltpu.make_async_remote_copy(
+            act.at[layer, x, 0], act.at[layer, x, 1],
+            act_ss.at[layer, x], act_rs.at[layer, x], device_id=partner, device_id_type=MESH,
+        )
+        act_own[layer][x].wait()
+        copy.start()
+        return copy
 
     def convolve(layer):
         copies = []
         for x in range(2):
             weight = wcat[layer] if x == 0 else wabs[layer]
             both = lax.dot_general(
-                cols[x], weight, (((1,), (1,)), ((), ())), preferred_element_type=F32
+                cols[layer, x], weight, (((1,), (1,)), ((), ())), preferred_element_type=F32
             )
-            part_own[x] = both[:, :128]
-            part_send[layer, x] = both[:, 128:].astype(BF16)
+            part_own[x] = jnp.where(lower, both[:, :128], both[:, 128:])
+            part_send[layer, x] = jnp.where(lower, both[:, 128:], both[:, :128]).astype(BF16)
             copy = pltpu.make_async_remote_copy(
                 part_send.at[layer, x], part_recv.at[layer, x],
                 part_ss.at[layer, x], part_rs.at[layer, x], device_id=partner, device_id_type=MESH,
             )
-            copy.start()
+            if layer == 1:
+                copy.start()
             copies.append(copy)
         return copies
 
     def turn_own(layer):
         for x in range(2):
-            act_t[x, :128, :] = act[layer, x, 0].T
+            act_t[layer, x, own_at, :] = act[layer, x, 0].T
 
     def kernel_terms(layer, copies):
         for x in range(2):
             copies[x].wait()
-            act_t[x, 128:, :] = act[layer, x, 1].T
-        for a in range(3):
-            at = pl.ds(384 * a, 384)
-            kc = jnp.dot(act_t[0], cols[0, :, at], preferred_element_type=F32)
-            kr = jnp.dot(act_t[1], cols[1, :, at], preferred_element_type=F32)
+            act_t[layer, x, other_at, :] = act[layer, x, 1].T
+        for i in range(3):
+            a = jnp.where(first, 2 - i, i)
+            at = pl.ds(pl.multiple_of(384 * a, 128), 384)
+            kc = jnp.dot(act_t[layer, 0], cols[layer, 0, :, at], preferred_element_type=F32)
+            kr = jnp.dot(act_t[layer, 1], cols[layer, 1, :, at], preferred_element_type=F32)
             w = wcat[layer, :, at].astype(F32)
             kr = jnp.where(w > 0.0, kr, jnp.where(w < 0.0, -kr, 0.0))
             k_full[layer, :, at] = scale * (kc + kr)
+            if i < 2:
+                core_copy(layer, i).start()
 
     def own_cols(which):
         return pl.ds(pl.multiple_of(which * 512, 512), 640)
@@ -255,14 +250,14 @@
     def rows_of(j):
         return pl.ds(pl.multiple_of(j * chunk, chunk), chunk)
 
-    def far_first(i, count):
-        k = lax.div(i + 1, 2)
-        return count // 2 + jnp.where(lax.rem(i, 2) == 1, k, -k)
-
-    def core_copy(layer):
-        return pltpu.make_async_remote_copy(
-            k_full.at[layer, :, own_cols(1 - core)], k_recv.at[layer],
-            core_ss.at[layer], core_rs.at[layer], device_id=sibling, device_id_type=MESH,
+    def core_copy(layer, i):
+        size = (384, 256)[i]
+        src = jnp.where(first, (768, 512)[i], (0, 384)[i])
+        dst = jnp.where(first, (256, 0)[i], (0, 384)[i])
+        return pltpu.make_async_remote_copy(
+            k_full.at[layer, :, pl.ds(pl.multiple_of(src, 128), size)],
+            k_recv.at[layer, :, pl.ds(pl.multiple_of(dst, 128), size)],
+            core_ss.at[layer, i], core_rs.at[layer, i], device_id=sibling, device_id_type=MESH,
         )
 
     def one_copy(layer, d):
@@ -288,15 +283,19 @@
             device_id=one_dev(j), device_id_type=MESH,
         )
 
+    def landed(layer, d):
+        j = lax.rem(pos_one - d + members, members)
+        return result.at[layer, core, rows_of(j), :]
+
     def back_from(layer, d):
-        there = result.at[layer, core, rows_of(lax.rem(pos_one - d + members, members)), :]
+        there = landed(layer, d)
         return pltpu.make_async_remote_copy(
             there, there, back_ss.at[layer, d - 1], back_rs.at[layer, d - 1],
             device_id=sibling, device_id_type=MESH,
         )
 
     def fwd_copy(layer, d):
-        there = result.at[layer, core, rows_of(lax.rem(pos_one - d + members, members)), :]
+        there = landed(layer, d)
         return pltpu.make_async_remote_copy(
             there, there, fwd_ss.at[layer, d], fwd_rs.at[layer, d],
             device_id=sibling, device_id_type=MESH,
@@ -310,7 +309,8 @@
         )
 
     def scatter(layer):
-        core_copy(layer).wait()
+        for i in range(2):
+            core_copy(layer, i).wait()
         own = k_full[layer, :, own_cols(core)]
         k_mine[layer] = (own + k_recv[layer]).astype(BF16)
 
@@ -354,12 +354,11 @@
 
     def write_out(layer, which):
         for tap in range(0, 5) if which == 0 else range(5, 9):
-            for half in range(2):
-                pltpu.make_async_copy(
-                    result.at[layer, which, pl.ds(128 * half, 128), pl.ds(128 * (tap - 4 * which), 128)],
-                    out_k.at[layer, tap, w_rows[half], :],
-                    k_out_sem.at[layer],
-                ).start()
+            pltpu.make_async_copy(
+                result.at[layer, which, :, pl.ds(128 * (tap - 4 * which), 128)],
+                out_k.at[layer, tap],
+                k_out_sem.at[layer],
+            ).start()
 
     def deliver(layer):
         @pl.loop(1, members)
@@ -382,24 +381,21 @@
         def _(d):
             fwd_copy(layer, d).wait_send()
 
-    place_inside(skip)
     pl.semaphore_wait(barrier, 4 + members - 1 + nz - 1)
     halo_two = send_halo(skip, 1)
-    act_two = send_act(1)
+    act_one_c = send_act(0, 0)
+    load_w(weight_two, 1)
+    place_inside(skip, 1)
+    load_w(weight_one, 0)
     wait_w(1)
     wabs[1] = jnp.abs(wcat[1])
-    turn_own(1)
     place_halo(halo_two, 1)
     part_two = convolve(1)
-    act_one = send_act(0)
-
-    kernel_terms(1, act_two)
-    core_copy(1).start()
+    act_one = (act_one_c, send_act(0, 1))
     turn_own(0)
     wait_w(0)
     wabs[0] = jnp.abs(wcat[0])
     s_one.wait()
-    scatter(1)
 
     for copy in part_two:
         copy.wait()
@@ -411,25 +407,32 @@
         inner[0, at, :] = ic
         inner[1, at, :] = ir
     halo_one = send_halo(inner, 0)
-    place_inside(inner)
+    act_two = (send_act(1, 0), send_act(1, 1))
+    place_inside(inner, 0)
+    turn_own(1)
     place_halo(halo_one, 0)
 
     kernel_terms(0, act_one)
-    core_copy(0).start()
+    scatter(0)
+
+    part_one = convolve(0)
+
+    kernel_terms(1, act_two)
+    scatter(1)
+    spread(0)
+    for copy in part_one:
+        copy.start()
     spread(1)
-    scatter(0)
-    part_one = convolve(0)
+    gather(0)
     gather(1)
-    spread(0)
 
     outs = []
     for x, out in enumerate((out_c, out_r)):
         part_one[x].wait()
         final[x] = skip[x].astype(F32) + part_own[x] + part_recv[0, x].astype(F32)
         outs.append(load(final.at[x], out, out_sem.at[x]))
+    deliver(0)
     deliver(1)
-    gather(0)
-    deliver(0)
     for copy in outs:
         copy.wait()
     for layer in range(2):
@@ -460,8 +463,6 @@
     flat = [a.reshape(pix, 128) for a in arrays[:6]]
     weights = [w.reshape(9, 256, 128) for w in arrays[6:8]]
     grads = [a.reshape(pix, 128) for a in arrays[8:]]
-    members = 2 * ny
-    chunk = 256 // members
     dma = pltpu.SemaphoreType.DMA
     out_c, out_r, out_k = pl.pallas_call(
         functools.partial(kernel, sizes),
@@ -479,11 +480,11 @@
             pltpu.VMEM((2, 256, 1152), BF16),
             pltpu.VMEM((2, 256, 1152), BF16),
             pltpu.VMEM((2, 2, 2, pix, 128), BF16),
-            pltpu.VMEM((2, 256, pix), BF16),
+            pltpu.VMEM((2, 2, 256, pix), BF16),
             pltpu.VMEM((2, pix, 128), BF16),
             pltpu.VMEM((2, pix, 128), BF16),
             pltpu.VMEM((2, 2, 2, width, 128), BF16),
-            pltpu.VMEM((2, pix, 1152), BF16),
+            pltpu.VMEM((2, 2, pix, 1152), BF16),
             pltpu.VMEM((2, pix, 128), F32),
             pltpu.VMEM((2, 2, pix, 128), BF16),
             pltpu.VMEM((2, 2, pix, 128), BF16),
@@ -491,9 +492,9 @@
             pltpu.VMEM((2, 256, 1152), F32),
             pltpu.VMEM((2, 256, 640), F32),
             pltpu.VMEM((2, 256, 640), BF16),
-            pltpu.VMEM((2, members, chunk, 640), BF16),
-            pltpu.VMEM((2, chunk, 640), BF16),
-            pltpu.VMEM((2, nz, chunk, 640), BF16),
+            pltpu.VMEM((2, 2 * ny, 128 // ny, 640), BF16),
+            pltpu.VMEM((2, 128 // ny, 640), BF16),
+            pltpu.VMEM((2, nz, 128 // ny, 640), BF16),
             pltpu.VMEM((2, 2, 256, 640), BF16),
             dma((4,)),
             dma((2,)),
@@ -504,16 +505,16 @@
             dma((2, 2)),
             dma((2, 2)),
             dma((2, 2)),
-            dma((2,)),
-            dma((2,)),
-            dma((2, members - 1)),
-            dma((2, members - 1)),
+            dma((2, 2)),
+            dma((2, 2)),
+            dma((2, 2 * ny - 1)),
+            dma((2, 2 * ny - 1)),
             dma((2, nz - 1)),
             dma((2, nz - 1)),
-            dma((2, members - 1)),
-            dma((2, members - 1)),
-            dma((2, members)),
-            dma((2, members)),
+            dma((2, 2 * ny - 1)),
+            dma((2, 2 * ny - 1)),
+            dma((2, 2 * ny)),
+            dma((2, 2 * ny)),
             dma((2,)),
             dma((2,)),
         ],

time: 77 us -> 74 us (0.961)
  Pallas kernels: 76.2 us -> 73.1 us
    pallas_call x1, Pallas kernels: 73.9 us -> 70.8 us  [body(): pl.pallas_call(functools.partial(kernel, sizes), name='interval_back', ou...]
where the time goes in v3:
time: 74 us; the launch traced here: 73.8 us
  Pallas kernels  73.1 us (99%)
    pallas_call x1, Pallas kernels, body(): pl.pallas_call(functools.partial(kernel, sizes), name='interval_back', ou...  70.8 us
    pallas_call x1, Pallas kernels, body(): pl.pallas_call(hand_over, name='hand_over', out_shape=(jax.ShapeDtypeStru...  2.3 us

profile of v3, /device:TPU:1, one launch (start us, length us, event | category | flops | bytes accessed | tf_op | source)
XLA Modules:
  0.0 73.8 jit_solution(439561298100977933)
XLA Ops:
  0.6 70.8 %interval_back.1 = (f32[512,128]{1,0:T(8,128)}, f32[512,128]{1,0:T(8,128)}, bf16[2,9,256,128]{3,2,1,0:T(8,128)(2,1)}) custom-call(bf16[512,128]{1,0:T(8,128)(2,1)} %bitcast.18, bf16[512,128]{1,0:T(8,128)(2,1)} %bitcast.19, bf16[512,128]{1,0:T(8,128)(2,1)} %bitcast.20, bf16[512,128]{1,0:T(8,128)(2,1)} %bitcast.21, s32[512,128]{1,0:T(8,128)} %bitcast.16, ...), custom_call_target="tpu_custom_call" | custom-call | tf_op jit(solution)/shard_map/interval_back/pallas_call | solution.py:467
  71.5 2.3 %hand_over.1 = (f32[512,128]{1,0:T(8,128)}, f32[512,128]{1,0:T(8,128)}, bf16[9,256,128]{2,1,0:T(8,128)(2,1)}, bf16[9,256,128]{2,1,0:T(8,128)(2,1)}) custom-call(f32[512,128]{1,0:T(8,128)} %get-tuple-element.11.made_c, f32[512,128]{1,0:T(8,128)} %get-tuple-element.12.made_r, bf16[2,9,256,128]{3,2,1,0:T(8,128)(2,1)} %get-tuple-element.13.made_k), custom_call_target="tpu_custom_call" | custom-call | tf_op jit(solution)/shard_map/hand_over/pallas_call | solution.py:526

commit v4 on v3

--- a/solution.py
+++ b/solution.py
@@ -360,12 +360,17 @@
                 k_out_sem.at[layer],
             ).start()
 
-    def deliver(layer):
-        @pl.loop(1, members)
-        def _(d):
+    def forward(layer):
+        @pl.loop(0, members - 1)
+        def _(i):
+            d = far_last(i)
             back_from(layer, d).wait_recv()
             fwd_copy(layer, d).start()
 
+    def far_last(i):
+        return far_first(members - 2 - i, members)
+
+    def finish(layer):
         @pl.loop(0, members)
         def _(d):
             fwd_from(layer, d).wait_recv()
@@ -373,6 +378,7 @@
         write_out(layer, 0)
         write_out(layer, 1)
 
+    def drain(layer):
         @pl.loop(1, members)
         def _(d):
             back_copy(layer, d).wait_send()
@@ -416,12 +422,12 @@
     scatter(0)
 
     part_one = convolve(0)
+    part_one[0].start()
 
     kernel_terms(1, act_two)
     scatter(1)
     spread(0)
-    for copy in part_one:
-        copy.start()
+    part_one[1].start()
     spread(1)
     gather(0)
     gather(1)
@@ -431,8 +437,12 @@
         part_one[x].wait()
         final[x] = skip[x].astype(F32) + part_own[x] + part_recv[0, x].astype(F32)
         outs.append(load(final.at[x], out, out_sem.at[x]))
-    deliver(0)
-    deliver(1)
+    forward(0)
+    forward(1)
+    finish(0)
+    finish(1)
+    drain(0)
+    drain(1)
     for copy in outs:
         copy.wait()
     for layer in range(2):

time: 74 us -> 74 us (level)
  no operation moved by 1% of the time
where the time goes in v4:
time: 74 us; the launch traced here: 73.8 us
  Pallas kernels  73.1 us (99%)
    pallas_call x1, Pallas kernels, body(): pl.pallas_call(functools.partial(kernel, sizes), name='interval_back', ou...  70.8 us
    pallas_call x1, Pallas kernels, body(): pl.pallas_call(hand_over, name='hand_over', out_shape=(jax.ShapeDtypeStru...  2.3 us

profile of v4, /device:TPU:1, one launch (start us, length us, event | category | flops | bytes accessed | tf_op | source)
XLA Modules:
  0.0 73.8 jit_solution(7314314858508039972)
XLA Ops:
  0.6 70.8 %interval_back.1 = (f32[512,128]{1,0:T(8,128)}, f32[512,128]{1,0:T(8,128)}, bf16[2,9,256,128]{3,2,1,0:T(8,128)(2,1)}) custom-call(bf16[512,128]{1,0:T(8,128)(2,1)} %bitcast.18, bf16[512,128]{1,0:T(8,128)(2,1)} %bitcast.19, bf16[512,128]{1,0:T(8,128)(2,1)} %bitcast.20, bf16[512,128]{1,0:T(8,128)(2,1)} %bitcast.21, s32[512,128]{1,0:T(8,128)} %bitcast.16, ...), custom_call_target="tpu_custom_call" | custom-call | tf_op jit(solution)/shard_map/interval_back/pallas_call | solution.py:477
  71.5 2.3 %hand_over.1 = (f32[512,128]{1,0:T(8,128)}, f32[512,128]{1,0:T(8,128)}, bf16[9,256,128]{2,1,0:T(8,128)(2,1)}, bf16[9,256,128]{2,1,0:T(8,128)(2,1)}) custom-call(f32[512,128]{1,0:T(8,128)} %get-tuple-element.11.made_c, f32[512,128]{1,0:T(8,128)} %get-tuple-element.12.made_r, bf16[2,9,256,128]{3,2,1,0:T(8,128)(2,1)} %get-tuple-element.13.made_k), custom_call_target="tpu_custom_call" | custom-call | tf_op jit(solution)/shard_map/hand_over/pallas_call | solution.py:536

commit v5 on v3

--- a/solution.py
+++ b/solution.py
@@ -366,12 +366,25 @@
             back_from(layer, d).wait_recv()
             fwd_copy(layer, d).start()
 
+        @pl.when(first)
+        def _():
+            write_out(layer, 0)
+
+        @pl.when(core == 1)
+        def _():
+            write_out(layer, 1)
+
         @pl.loop(0, members)
         def _(d):
             fwd_from(layer, d).wait_recv()
 
-        write_out(layer, 0)
-        write_out(layer, 1)
+        @pl.when(first)
+        def _():
+            write_out(layer, 1)
+
+        @pl.when(core == 1)
+        def _():
+            write_out(layer, 0)
 
         @pl.loop(1, members)
         def _(d):
@@ -415,10 +428,9 @@
     kernel_terms(0, act_one)
     scatter(0)
 
-    part_one = convolve(0)
-
     kernel_terms(1, act_two)
     scatter(1)
+    part_one = convolve(0)
     spread(0)
     for copy in part_one:
         copy.start()
@@ -440,21 +452,29 @@
 
 
 def hand_over(made_c, made_r, made_k, out_c, out_r, out_one, out_two, wide, taps, load_sem, sem):
-    sources = (made_c, made_r, made_k.at[0], made_k.at[1])
-    buffers = (wide.at[0], wide.at[1], taps.at[0], taps.at[1])
-    targets = (out_c, out_r, out_one, out_two)
+    half = wide.shape[1] // 2
     loads = []
     stores = []
-    for i in range(4):
-        loads.append(pltpu.make_async_copy(sources[i], buffers[i], load_sem.at[i]))
-        stores.append(pltpu.make_async_copy(buffers[i], targets[i], sem.at[i]))
-    for copy in loads:
-        copy.start()
-    for i in range(4):
-        loads[i].wait()
-        stores[i].start()
-    for copy in stores:
-        copy.wait()
+
+    def add(source, buffer, target):
+        i = len(loads)
+        loads.append(pltpu.make_async_copy(source, buffer, load_sem.at[i]))
+        stores.append(pltpu.make_async_copy(buffer, target, sem.at[i]))
+        loads[i].start()
+
+    for layer, target in enumerate((out_one, out_two)):
+        for part in range(3):
+            at = pl.ds(3 * part, 3)
+            add(made_k.at[layer, at], taps.at[layer, at], target.at[at])
+    for i, (source, target) in enumerate(((made_c, out_c), (made_r, out_r))):
+        for part in range(2):
+            at = pl.ds(half * part, half)
+            add(source.at[at], wide.at[i, at], target.at[at])
+    for load, store in zip(loads, stores):
+        load.wait()
+        store.start()
+    for store in stores:
+        store.wait()
 
 
 def body(sizes, *arrays):
@@ -537,8 +557,8 @@
         scratch_shapes=[
             pltpu.VMEM((2, pix, 128), F32),
             pltpu.VMEM((2, 9, 256, 128), BF16),
-            dma((4,)),
-            dma((4,)),
+            dma((10,)),
+            dma((10,)),
         ],
         compiler_params=pltpu.CompilerParams(vmem_limit_bytes=62 << 20),
     )(out_c, out_r, out_k)

time: 74 us -> 74 us (level)
  no operation moved by 1% of the time
where the time goes in v5:
time: 74 us; the launch traced here: 73.7 us
  Pallas kernels  73.1 us (99%)
    pallas_call x1, Pallas kernels, body(): pl.pallas_call(functools.partial(kernel, sizes), name='interval_back', ou...  70.7 us
    pallas_call x1, Pallas kernels, body(): pl.pallas_call(hand_over, name='hand_over', out_shape=(jax.ShapeDtypeStru...  2.37 us

profile of v5, /device:TPU:1, one launch (start us, length us, event | category | flops | bytes accessed | tf_op | source)
XLA Modules:
  0.0 73.7 jit_solution(18182242255919464692)
XLA Ops:
  0.6 70.7 %interval_back.1 = (f32[512,128]{1,0:T(8,128)}, f32[512,128]{1,0:T(8,128)}, bf16[2,9,256,128]{3,2,1,0:T(8,128)(2,1)}) custom-call(bf16[512,128]{1,0:T(8,128)(2,1)} %bitcast.18, bf16[512,128]{1,0:T(8,128)(2,1)} %bitcast.19, bf16[512,128]{1,0:T(8,128)(2,1)} %bitcast.20, bf16[512,128]{1,0:T(8,128)(2,1)} %bitcast.21, s32[512,128]{1,0:T(8,128)} %bitcast.16, ...), custom_call_target="tpu_custom_call" | custom-call | tf_op jit(solution)/shard_map/interval_back/pallas_call | solution.py:487
  71.4 2.4 %hand_over.1 = (f32[512,128]{1,0:T(8,128)}, f32[512,128]{1,0:T(8,128)}, bf16[9,256,128]{2,1,0:T(8,128)(2,1)}, bf16[9,256,128]{2,1,0:T(8,128)(2,1)}) custom-call(f32[512,128]{1,0:T(8,128)} %get-tuple-element.11.made_c, f32[512,128]{1,0:T(8,128)} %get-tuple-element.12.made_r, bf16[2,9,256,128]{3,2,1,0:T(8,128)(2,1)} %get-tuple-element.13.made_k), custom_call_target="tpu_custom_call" | custom-call | tf_op jit(solution)/shard_map/hand_over/pallas_call | solution.py:546
